TPU v7x, 32 devices: a whole 2x2x4 slice. The times are simulated.
32 devices in a mesh: section: 16 (over z, x, core), expert: 2 (over y).
Axes of the slice: x: 2, y: 2, z: 4, core: 2. Of those that a mesh axis runs over, the one named last changes fastest.
Arguments:
- tokens: bfloat16 [128, 3072], P('expert', 'section'), may hold values from -6 to 6
- routes: int32 [128, 2], P('expert'), may hold values from 0 to 7, all different within a row; in each aligned block of 64 rows (0 to 63, 64 to 127, ...) at most 20 rows name the same one
- combine: float32 [128, 2], P('expert'), may hold values from 0.1 to 1
- w_gate: bfloat16 [8, 3072, 8192], P('expert', None, 'section'), may hold values from -0.109375 to 0.109375
- w_up: bfloat16 [8, 3072, 8192], P('expert', None, 'section'), may hold values from -0.109375 to 0.109375
- w_down: bfloat16 [8, 8192, 3072], P('expert', 'section'), may hold values from -0.0625 to 0.0625
- cotangent: bfloat16 [128, 3072], P('expert', 'section'), may hold values from -6 to 6
Outputs:
- mixed: bfloat16 [128, 3072], P('expert', 'section')
- d_tokens: bfloat16 [128, 3072], P('expert', 'section')
- d_combine: float32 [128, 2], P('expert')
- grad_gate: bfloat16 [8, 3072, 8192], P('expert', None, 'section')
- grad_up: bfloat16 [8, 3072, 8192], P('expert', None, 'section')
- grad_down: bfloat16 [8, 8192, 3072], P('expert', 'section')
Inputs may be any that keep to these rules, and one draw needn't show every extreme that they name: `routes`: each row names 2 different experts. In the 64 rows held by one index of the `expert` axis, no expert is named more than 20 times.
All inputs are finite; a program needn't handle non-finite values.
Results may differ from a plain program's by a relative error of at most 0.0065.
Values may be sent and summed in bfloat16 or wider, within the bound.
A program may use at most 192 MiB of HBM per device.

v0:
```python
import jax
import jax.numpy as jnp
from jax import lax
from jax.sharding import PartitionSpec as P

TOPK = 2
CAP = 20


def on_device(tokens, routes, combine, w_gate, w_up, w_down, cotangent):
    groups = lax.axis_size("expert")
    tok_rows = tokens.shape[0]
    local = w_gate.shape[0]
    experts_all = local * groups
    slots_all = experts_all * CAP
    feat_local = tokens.shape[1]
    flat_ids = routes.reshape(-1)
    onehot = (flat_ids[:, None] == jnp.arange(experts_all, dtype=jnp.int32)[None, :]).astype(
        jnp.int32
    )
    earlier = jnp.cumsum(onehot, axis=0) - onehot
    slot = jnp.sum(earlier * onehot, axis=1)
    target = flat_ids * CAP + slot
    places = (target[:, None] == jnp.arange(slots_all, dtype=jnp.int32)[None, :]).astype(
        jnp.float32
    )
    places_three = places.reshape(tok_rows, TOPK, slots_all)
    picker = jnp.sum(places_three, axis=1).astype(jnp.bfloat16)
    slot_weight = jnp.sum(places_three * combine[:, :, None], axis=(0, 1))
    places_half = places.astype(jnp.bfloat16)

    def spread(values, scaling):
        whole = lax.all_gather(values, "section", axis=1, tiled=True)
        sent = jnp.dot(picker.T, whole, preferred_element_type=jnp.float32)
        if scaling is not None:
            sent = sent * scaling[:, None]
        sent = sent.astype(jnp.bfloat16).reshape(experts_all, CAP, whole.shape[1])
        return lax.all_to_all(sent, "expert", split_axis=0, concat_axis=1, tiled=True)

    def collect(term):
        shaped = term.reshape(feat_local, local, groups, CAP)
        back = lax.all_to_all(shaped, "expert", split_axis=2, concat_axis=1, tiled=True)
        back = back.reshape(feat_local, slots_all)
        picked = jnp.einsum("af,df->ad", places_half, back, preferred_element_type=jnp.float32)
        return picked.reshape(tok_rows, TOPK, feat_local)

    expert_in = spread(tokens, None)
    gate = jnp.einsum("erd,edh->erh", expert_in, w_gate, preferred_element_type=jnp.float32)
    up = jnp.einsum("erd,edh->erh", expert_in, w_up, preferred_element_type=jnp.float32)
    sig = jax.nn.sigmoid(gate)
    act = gate * sig
    hidden = (act * up).astype(jnp.bfloat16)
    expert_out = lax.psum_scatter(
        jnp.einsum("erh,ehd->der", hidden, w_down, preferred_element_type=jnp.float32),
        "section",
        scatter_dimension=0,
        tiled=True,
    ).astype(jnp.bfloat16)
    rows = collect(expert_out)
    mixed = jnp.sum(combine[:, :, None] * rows, axis=1).astype(jnp.bfloat16)
    cot = cotangent.astype(jnp.float32)
    d_combine = lax.psum(jnp.sum(rows * cot[:, None, :], axis=2), "section")
    d_out = spread(cotangent, slot_weight)
    d_hidden = jnp.einsum("erd,ehd->erh", d_out, w_down, preferred_element_type=jnp.float32)
    d_gate = (d_hidden * up * sig * (1.0 + gate * (1.0 - sig))).astype(jnp.bfloat16)
    d_up = (d_hidden * act).astype(jnp.bfloat16)
    grad_down = jnp.einsum(
        "erh,erd->ehd", hidden, d_out, preferred_element_type=jnp.float32
    ).astype(jnp.bfloat16)
    grad_gate = jnp.einsum(
        "erd,erh->edh", expert_in, d_gate, preferred_element_type=jnp.float32
    ).astype(jnp.bfloat16)
    grad_up = jnp.einsum(
        "erd,erh->edh", expert_in, d_up, preferred_element_type=jnp.float32
    ).astype(jnp.bfloat16)
    first = jnp.einsum("erh,edh->der", d_gate, w_gate, preferred_element_type=jnp.float32)
    second = jnp.einsum("erh,edh->der", d_up, w_up, preferred_element_type=jnp.float32)
    d_in = lax.psum_scatter(first + second, "section", scatter_dimension=0, tiled=True).astype(
        jnp.bfloat16
    )
    back_rows = collect(d_in)
    d_tokens = jnp.sum(back_rows, axis=1).astype(jnp.bfloat16)
    return (mixed, d_tokens, d_combine, grad_gate, grad_up, grad_down)


def solution(mesh):
    placed = (
        P("expert", "section"),
        P("expert", None),
        P("expert", None),
        P("expert", None, "section"),
        P("expert", None, "section"),
        P("expert", "section", None),
        P("expert", "section"),
    )
    return jax.shard_map(
        on_device,
        mesh=mesh,
        in_specs=placed,
        out_specs=(
            P("expert", "section"),
            P("expert", "section"),
            P("expert", None),
            P("expert", None, "section"),
            P("expert", None, "section"),
            P("expert", "section", None),
        ),
        check_vma=False,
    )
```

profile of v0, /device:TPU:0, one launch (start us, length us, event | category | flops | bytes accessed | tf_op | source)
XLA Modules:
  0.0 303.2 jit_solution(3782347542082900483)
XLA Ops:
  7.2 0.8 copy.79
  7.9 0.1 eq.54
  8.1 0.1 fusion.17
  8.2 0.2 reduce_window_sum.11
  8.3 0.2 select_reduce_fusion.1
  8.5 0.1 reduce_sum.57
  8.7 0.1 copy.80
  8.7 0.7 multiply_add_fusion
  9.4 24.8 %all-gather.1 = bf16[16,192,64]{1,2,0:T(8,128)(2,1)S(1)} all-gather(bf16[1,192,64]{1,2,0:T(8,128)(2,1)} %bitcast.80), channel_id=1, replica_groups=mesh['section'=16,'expert'=2] {'section'}, dimensions={0}, use_global_device_ids=true | all-gather | bytes 417792 | tf_op jit(solution)/shard_map/all_gather | solution.py:33
  34.2 0.3 copy.87
  34.5 0.5 reshape.108
  35.1 0.8 select_reduce_fusion
  35.9 0.4 fusion
  36.3 1.1 reshape.102
  37.4 3.6 %all-to-all-start.2 = ((bf16[8,20,3072]{2,1,0:T(8,128)(2,1)}), bf16[8,20,3072]{2,1,0:T(8,128)(2,1)S(1)}, u32[]{:S(2)}, u32[]{:S(2)}) async-start(bf16[8,20,3072]{2,1,0:T(8,128)(2,1)} %reshape.102), calls=%async_computation.2 | async-start | bytes 2359296 | tf_op jit(solution)/shard_map/all_to_all | solution.py:38
  41.0 19.1 %all-gather = bf16[16,192,64]{1,2,0:T(8,128)(2,1)S(1)} all-gather(bf16[1,192,64]{1,2,0:T(8,128)(2,1)} %bitcast.81), channel_id=1, replica_groups=mesh['section'=16,'expert'=2] {'section'}, dimensions={0}, use_global_device_ids=true | all-gather | bytes 417792 | tf_op jit(solution)/shard_map/all_gather | solution.py:33
  60.2 0.3 copy.81
  60.5 0.5 reshape.106
  61.0 0.4 convolution_convert_fusion.3
  61.5 1.1 reshape.99
  62.6 0.0 all-to-all-done.2
  62.6 3.6 %all-to-all-start = ((bf16[8,20,3072]{2,1,0:T(8,128)(2,1)}), bf16[8,20,3072]{2,1,0:T(8,128)(2,1)S(1)}, u32[]{:S(2)}, u32[]{:S(2)}) async-start(bf16[8,20,3072]{2,1,0:T(8,128)(2,1)} %reshape.99), calls=%async_computation | async-start | bytes 2359296 | tf_op jit(solution)/shard_map/all_to_all | solution.py:38
  66.2 0.2 reduce-scatter.9.cloned.1.call-start
  66.4 0.8 copy.88
  67.2 14.8 %all-to-all-done = bf16[8,20,3072]{2,1,0:T(8,128)(2,1)S(1)} async-done(((bf16[8,20,3072]{2,1,0:T(8,128)(2,1)}), bf16[8,20,3072]{2,1,0:T(8,128)(2,1)S(1)}, u32[]{:S(2)}, u32[]{:S(2)}) %all-to-all-start) | async-done | bytes 983072 | tf_op jit(solution)/shard_map/all_to_all | solution.py:38
  82.0 1.0 copy-done.1
  83.1 2.2 copy.82
  85.2 0.0 slice-start
  85.3 0.0 slice-start.1
  85.3 8.0 %fusion.6 = f32[4,40,512]{2,1,0:T(8,128)} fusion(bf16[4,3072,512]{2,1,0:T(8,128)(2,1)} %param.11, bf16[4,40,3072]{2,0,1:T(4,128)(2,1)S(1)} %bitcast.66), kind=kOutput, calls=%fused_computation.13 | convolution fusion | flops 503316480 | bytes 13893632 | tf_op jit(solution)/shard_map/erd,edh->erh/dot_general | solution.py:49
  93.3 0.0 copy-done
  93.3 2.7 fusion.8
  96.0 0.0 slice-done
  96.0 0.0 slice-done.1
  96.0 0.0 slice-done.2
  96.0 5.8 %multiply_convert_fusion = (bf16[4,40,512]{2,1,0:T(8,128)(2,1)}, bf16[4,40,512]{2,1,0:T(8,128)(2,1)}, bf16[4,40,512]{2,1,0:T(8,128)(2,1)}) fusion(f32[4,40,512]{2,1,0:T(8,128)} %fusion.8, f32[4,40,512]{2,1,0:T(8,128)} %fusion.6, bf16[4,512,3072]{2,1,0:T(8,128)(2,1)S(1)} %bitcast.65, bf16[4,40,3072]{2,0,1:T(4,128)(2,1)S(1)} %bitcast.70), kind=kOutput, calls=%fused_computation.17 | convolution fusion | flops 504545280 | bytes 14712832 | tf_op jit(solution)/shard_map/erd,ehd->erh/dot_general | solution.py:64
  101.8 8.5 %fusion.21 = f32[4,40,3072]{2,1,0:T(8,128)S(1)} fusion(bf16[4,40,512]{2,1,0:T(8,128)(2,1)} %get-tuple-element.11, bf16[4,3072,512]{2,1,0:T(8,128)(2,1)} %param.10), kind=kOutput, calls=%fused_computation.40 | convolution fusion | flops 503316480 | bytes 14712832 | tf_op jit(solution)/shard_map/erh,edh->der/dot_general | solution.py:76
  110.3 0.0 copy-done.3
  110.3 0.0 copy-start.4
  110.3 9.6 %convolution_add_fusion = f32[4,40,3072]{2,1,0:T(8,128)} fusion(f32[4,40,3072]{2,1,0:T(8,128)S(1)} %fusion.21, bf16[4,40,512]{2,1,0:T(8,128)(2,1)S(1)} %copy-done.3, bf16[4,3072,512]{2,1,0:T(8,128)(2,1)} %param.11), kind=kOutput, calls=%fused_computation.3 | convolution fusion | flops 503808000 | bytes 16678912 | tf_op jit(solution)/shard_map/erh,edh->der/dot_general | solution.py:77
  120.0 3.3 %copy.101 = f32[3072,160]{1,0:T(8,128)} copy(f32[3072,160]{0,1:T(8,128)} %bitcast.72) | data formatting | bytes 3932160
  123.3 0.0 reduce-scatter.9.cloned.1.call-update
  123.3 0.3 reduce-scatter.7.cloned.1.call-start
  123.6 0.0 copy-done.4
  123.6 8.3 %fusion.20 = f32[4,40,3072]{2,1,0:T(8,128)} fusion(bf16[4,40,512]{2,1,0:T(8,128)(2,1)S(1)} %copy-done.4, bf16[4,512,3072]{2,1,0:T(8,128)(2,1)} %param.12), kind=kOutput, calls=%fused_computation.39 | convolution fusion | flops 503316480 | bytes 14712832 | tf_op jit(solution)/shard_map/erh,ehd->der/dot_general | solution.py:54
  131.9 3.4 %copy.99 = f32[3072,160]{1,0:T(8,128)} copy(f32[3072,160]{0,1:T(8,128)} %bitcast.73) | data formatting | bytes 3932160
  135.3 0.0 reduce-scatter.7.cloned.1.call-update
  135.3 0.0 copy-done.5
  135.3 6.7 %convolution_convert_fusion = bf16[4,512,3072]{2,1,0:T(8,128)(2,1)} fusion(bf16[4,40,512]{2,1,0:T(8,128)(2,1)S(1)} %copy-done.4, bf16[4,40,3072]{2,0,1:T(4,128)(2,1)S(1)} %bitcast.71), kind=kOutput, calls=%fused_computation | convolution fusion | flops 509607936 | bytes 13729792 | tf_op jit(solution)/shard_map/erh,erd->ehd/dot_general | solution.py:67
  142.0 6.6 %convolution_convert_fusion.1 = bf16[4,3072,512]{2,1,0:T(8,128)(2,1)} fusion(bf16[4,40,512]{2,1,0:T(8,128)(2,1)S(1)} %copy-done.3, bf16[4,40,3072]{2,0,1:T(4,128)(2,1)S(1)} %bitcast.68), kind=kOutput, calls=%fused_computation.1 | convolution fusion | flops 509607936 | bytes 13729792 | tf_op jit(solution)/shard_map/erd,erh->edh/dot_general | solution.py:73
  148.6 38.7 %reduce-scatter.9.cloned.1.call-done = f32[192,160]{1,0:T(8,128)} async-done(((f32[3072,160]{1,0:T(8,128)}), f32[192,160]{1,0:T(8,128)}) %reduce-scatter.9.cloned.1.call-update) | async-done | bytes 122896
  187.3 1.0 copy.102
  188.3 0.7 copy.90
  189.0 3.3 %all-to-all-start.3 = ((bf16[192,4,2,20]{0,1,3,2:T(4,128)(2,1)}), bf16[192,4,2,20]{0,1,3,2:T(4,128)(2,1)S(1)}, u32[]{:S(2)}, u32[]{:S(2)}) async-start(bf16[192,4,2,20]{0,1,3,2:T(4,128)(2,1)} %bitcast.17), calls=%async_computation.3 | async-start | bytes 163840 | tf_op jit(solution)/shard_map/all_to_all | solution.py:42
  192.3 6.6 %convolution_convert_fusion.2 = bf16[4,3072,512]{2,1,0:T(8,128)(2,1)} fusion(bf16[4,40,512]{2,1,0:T(8,128)(2,1)S(1)} %copy-done.2, bf16[4,40,3072]{2,0,1:T(4,128)(2,1)S(1)} %bitcast.69), kind=kOutput, calls=%fused_computation.2 | convolution fusion | flops 509607936 | bytes 13729792 | tf_op jit(solution)/shard_map/erd,erh->edh/dot_general | solution.py:70
  198.9 57.3 %reduce-scatter.7.cloned.1.call-done = f32[192,160]{1,0:T(8,128)} async-done(((f32[3072,160]{1,0:T(8,128)}), f32[192,160]{1,0:T(8,128)}) %reduce-scatter.7.cloned.1.call-update) | async-done | bytes 122896
  256.3 1.0 copy.100
  257.3 0.7 copy.85
  258.0 0.0 all-to-all-done.3
  258.0 3.3 %all-to-all-start.1 = ((bf16[192,4,2,20]{0,1,3,2:T(4,128)(2,1)}), bf16[192,4,2,20]{0,1,3,2:T(4,128)(2,1)S(1)}, u32[]{:S(2)}, u32[]{:S(2)}) async-start(bf16[192,4,2,20]{0,1,3,2:T(4,128)(2,1)} %bitcast.8), calls=%async_computation.1 | async-start | bytes 163840 | tf_op jit(solution)/shard_map/all_to_all | solution.py:42
  261.3 0.8 convolution_reduce_fusion
  262.2 3.3 %all-to-all-done.1 = bf16[192,4,2,20]{0,1,3,2:T(4,128)(2,1)S(1)} async-done(((bf16[192,4,2,20]{0,1,3,2:T(4,128)(2,1)}), bf16[192,4,2,20]{0,1,3,2:T(4,128)(2,1)S(1)}, u32[]{:S(2)}, u32[]{:S(2)}) %all-to-all-start.1) | async-done | bytes 61472 | tf_op jit(solution)/shard_map/all_to_all | solution.py:42
  265.5 0.8 multiply_reduce_fusion
  266.4 30.0 %psum.7 = f32[64,2]{0,1:T(2,128)} all-reduce(f32[64,2]{0,1:T(2,128)S(1)} %get-tuple-element.6), channel_id=1, replica_groups=mesh['section'=16,'expert'=2] {'section'}, use_global_device_ids=true, to_apply=%region_9.10 | all-reduce | flops 128 | bytes 1024 | tf_op jit(solution)/shard_map/psum | solution.py:62
  (15 shorter events, 0.1 us)
Async XLA Ops:
  37.4 25.2 %all-to-all-start.2 = ((bf16[8,20,3072]{2,1,0:T(8,128)(2,1)}), bf16[8,20,3072]{2,1,0:T(8,128)(2,1)S(1)}, u32[]{:S(2)}, u32[]{:S(2)}) async-start(bf16[8,20,3072]{2,1,0:T(8,128)(2,1)} %reshape.102), calls=%async_computation.2 | async-start | bytes 2359296 | tf_op jit(solution)/shard_map/all_to_all | solution.py:38
  62.6 19.5 %all-to-all-start = ((bf16[8,20,3072]{2,1,0:T(8,128)(2,1)}), bf16[8,20,3072]{2,1,0:T(8,128)(2,1)S(1)}, u32[]{:S(2)}, u32[]{:S(2)}) async-start(bf16[8,20,3072]{2,1,0:T(8,128)(2,1)} %reshape.99), calls=%async_computation | async-start | bytes 2359296 | tf_op jit(solution)/shard_map/all_to_all | solution.py:38
  66.2 121.1 %reduce-scatter.9.cloned.1.call-start = ((), (), s32[]{:S(2)}) async-start(), calls=%async_computation.7 | async-start | bytes 3342336
  82.0 1.0 copy-start.1
  83.1 10.2 %copy-start = (bf16[4,3072,512]{2,1,0:T(8,128)(2,1)S(1)}, bf16[4,3072,512]{2,1,0:T(8,128)(2,1)}, u32[]{:S(2)}) copy-start(bf16[4,3072,512]{2,1,0:T(8,128)(2,1)} %param.10) | copy-start | bytes 37748740
  85.2 10.8 %slice-start = ((s8[12582912]{0:T(1024)(128)(4,1)}), s8[4194304]{0:T(1024)(128)(4,1)S(1)}, s32[]{:S(2)}) async-start(s8[12582912]{0:T(1024)(128)(4,1)} %bitcast.64), calls=%async_computation.8 | async-start | bytes 8388608
  85.3 10.8 %slice-start.1 = ((s8[12582912]{0:T(1024)(128)(4,1)}), s8[4194304]{0:T(1024)(128)(4,1)S(1)}, s32[]{:S(2)}) async-start(s8[12582912]{0:T(1024)(128)(4,1)} %bitcast.64), calls=%async_computation.9 | async-start | bytes 8388608
  93.3 2.8 slice-start.2
  101.8 8.5 %copy-start.3 = (bf16[4,40,512]{2,1,0:T(8,128)(2,1)S(1)}, bf16[4,40,512]{2,1,0:T(8,128)(2,1)}, u32[]{:S(2)}) copy-start(bf16[4,40,512]{2,1,0:T(8,128)(2,1)} %get-tuple-element.10) | copy-start | bytes 491524
  110.3 13.3 %copy-start.4 = (bf16[4,40,512]{2,1,0:T(8,128)(2,1)S(1)}, bf16[4,40,512]{2,1,0:T(8,128)(2,1)}, u32[]{:S(2)}) copy-start(bf16[4,40,512]{2,1,0:T(8,128)(2,1)} %get-tuple-element.12) | copy-start | bytes 491524
  123.3 12.0 %copy-start.5 = (bf16[64,192]{1,0:T(8,128)(2,1)S(1)}, bf16[64,192]{1,0:T(8,128)(2,1)}, u32[]{:S(2)}) copy-start(bf16[64,192]{1,0:T(8,128)(2,1)} %param.13) | copy-start | bytes 73732
  123.3 133.0 %reduce-scatter.7.cloned.1.call-start = ((), (), s32[]{:S(2)}) async-start(), calls=%async_computation.6 | async-start | bytes 3342336
  142.0 50.3 %copy-start.2 = (bf16[4,40,512]{2,1,0:T(8,128)(2,1)S(1)}, bf16[4,40,512]{2,1,0:T(8,128)(2,1)}, u32[]{:S(2)}) copy-start(bf16[4,40,512]{2,1,0:T(8,128)(2,1)} %get-tuple-element.11) | copy-start | bytes 491524
  148.6 116.9 %copy-start.6 = (f32[64,2]{0,1:T(2,128)S(1)}, f32[64,2]{0,1:T(2,128)}, u32[]{:S(2)}) copy-start(f32[64,2]{0,1:T(2,128)} %param.9) | copy-start | bytes 1540
  189.0 69.0 %all-to-all-start.3 = ((bf16[192,4,2,20]{0,1,3,2:T(4,128)(2,1)}), bf16[192,4,2,20]{0,1,3,2:T(4,128)(2,1)S(1)}, u32[]{:S(2)}, u32[]{:S(2)}) async-start(bf16[192,4,2,20]{0,1,3,2:T(4,128)(2,1)} %bitcast.17), calls=%async_computation.3 | async-start | bytes 163840 | tf_op jit(solution)/shard_map/all_to_all | solution.py:42
  258.0 7.5 %all-to-all-start.1 = ((bf16[192,4,2,20]{0,1,3,2:T(4,128)(2,1)}), bf16[192,4,2,20]{0,1,3,2:T(4,128)(2,1)S(1)}, u32[]{:S(2)}, u32[]{:S(2)}) async-start(bf16[192,4,2,20]{0,1,3,2:T(4,128)(2,1)} %bitcast.8), calls=%async_computation.1 | async-start | bytes 163840 | tf_op jit(solution)/shard_map/all_to_all | solution.py:42
Sparse Core Ops, SparseCore 0:
  123.4 63.8 reduce-scatter.8
  191.1 65.1 reduce-scatter.6
where the time goes:
time: 304 us; the launch traced here: 303 us
  waiting for transfers between devices  114 us (38%)
  blocking collectives  73.9 us (24%)
  matrix products  65.4 us (22%)
  local copies, waits for them, and re-layouts  19.2 us (6%)
  starting transfers between devices  14.3 us (5%)
  between operations  14.3 us (5%)
    unnamed x4, waiting for transfers between devices  96 us
    all_gather x2, blocking collectives, spread(): whole = lax.all_gather(values, 'section', axis=1, tiled=True)  43.9 us
    psum x1, blocking collectives, on_device(): d_combine = lax.psum(jnp.sum(rows * cot[:, None, :], axis=2), 'section')  30 us
    all_to_all x2, waiting for transfers between devices, spread(): lax.all_to_all(sent, 'expert', split_axis=0, concat_axis=1, tiled=True)  14.8 us
    unnamed x27, local copies, waits for them, and re-layouts  11.7 us
    dot_general x1, matrix products, on_device(): jnp.einsum('erh,edh->der', d_up, w_up, preferred_element_type=jnp.float32)  9.64 us
    dot_general x1, matrix products, on_device(): jnp.einsum('erh,edh->der', d_gate, w_gate, preferred_element_type=jnp.flo...  8.45 us
    dot_general x1, matrix products, on_device(): jnp.einsum('erh,ehd->der', hidden, w_down, preferred_element_type=jnp.flo...  8.31 us
  transfers between devices with their start and end apart: 6, of which 4 were waited for; matrix products, arithmetic and copies ran while one was open for 13% of the time, Pallas kernels for 0%

commit v1 on v0

v1 whole, which is shorter than its diff:
```python
import functools
import math

import jax
import jax.numpy as jnp
from jax import lax
from jax.experimental import pallas as pl
from jax.experimental.pallas import tpu as pltpu
from jax.sharding import PartitionSpec as P

TOPK = 2
CAP = 20
MESH = pl.DeviceIdType.MESH
EX, HI, MID, LOW = 0, 1, 2, 3
ORDERS = ((HI, MID, EX, LOW), (EX, HI, MID, LOW))


def sizes_of(groups, section):
    return (groups, section // 4, 2, 2)


def place():
    sec = lax.axis_index("section")
    return (
        lax.axis_index("expert"),
        lax.div(sec, 4),
        lax.rem(lax.div(sec, 2), 2),
        lax.rem(sec, 2),
    )


def peer(me, sizes, dim, step):
    there = list(me)
    there[dim] = lax.rem(me[dim] + step, sizes[dim])
    return tuple(there)


def device(where):
    return {"expert": where[EX], "section": (where[HI] * 2 + where[MID]) * 2 + where[LOW]}


def greet(me, sizes):
    barrier = pltpu.get_barrier_semaphore()
    count = 0
    for dim in range(4):
        for step in range(1, sizes[dim]):
            pl.semaphore_signal(
                barrier, inc=1, device_id=device(peer(me, sizes, dim, step)), device_id_type=MESH
            )
            count += 1
    pl.semaphore_wait(barrier, count)


def split_rows(rows):
    if rows % 32 == 0:
        return ((0, rows // 2), (rows // 2, rows // 2))
    return ((0, rows),)


def gather_kernel(sizes, parts, x_ref, info_ref, out_ref, info_out, send, recv, isend, irecv):
    me = place()
    out_ref[me[0], me[1], me[2], me[3]] = x_ref[...]
    info_out[me[EX]] = info_ref[...]
    greet(me, sizes)
    copies = []
    for step in range(1, sizes[EX]):
        copy = pltpu.make_async_remote_copy(
            src_ref=info_ref,
            dst_ref=info_out.at[me[EX]],
            send_sem=isend.at[step - 1],
            recv_sem=irecv.at[step - 1],
            device_id=device(peer(me, sizes, EX, step)),
            device_id_type=MESH,
        )
        copy.start()
        copies.append(copy)
    have = [list(me) for _ in parts]
    before = [[] for _ in parts]
    for stage in range(4):
        for p, (low, rows) in enumerate(parts):
            for copy in before[p]:
                copy.wait_recv()
            dim = ORDERS[p][stage]
            block = out_ref.at[tuple(have[p]) + (pl.ds(low, rows),)]
            before[p] = []
            for step in range(1, sizes[dim]):
                copy = pltpu.make_async_remote_copy(
                    src_ref=block,
                    dst_ref=block,
                    send_sem=send.at[p, stage, step - 1],
                    recv_sem=recv.at[p, stage, step - 1],
                    device_id=device(peer(me, sizes, dim, step)),
                    device_id_type=MESH,
                )
                copy.start()
                before[p].append(copy)
                copies.append(copy)
            have[p][dim] = pl.ds(0, sizes[dim])
    for p in range(len(parts)):
        for copy in before[p]:
            copy.wait_recv()
    for copy in copies[: sizes[EX] - 1]:
        copy.wait_recv()
    for copy in copies:
        copy.wait_send()


def gather(block, info, sizes):
    rows = block.shape[0]
    parts = split_rows(rows)
    most = max(sizes) - 1
    vmem = pl.BlockSpec(memory_space=pltpu.VMEM)
    return pl.pallas_call(
        functools.partial(gather_kernel, sizes, parts),
        out_shape=(
            jax.ShapeDtypeStruct(sizes + block.shape, block.dtype),
            jax.ShapeDtypeStruct((sizes[EX],) + info.shape, info.dtype),
        ),
        in_specs=[vmem, vmem],
        out_specs=(vmem, vmem),
        scratch_shapes=[
            pltpu.SemaphoreType.DMA((len(parts), 4, most)),
            pltpu.SemaphoreType.DMA((len(parts), 4, most)),
            pltpu.SemaphoreType.DMA((most,)),
            pltpu.SemaphoreType.DMA((most,)),
        ],
        compiler_params=pltpu.CompilerParams(
            collective_id=0, has_side_effects=True, vmem_limit_bytes=40 * 2**20
        ),
    )(block, info)


def left_shape(sizes, order, stage):
    gone = order[: stage + 1]
    return tuple(1 if d in gone else sizes[d] for d in range(4))


def scatter_kernel(sizes, parts, p_ref, out_ref, acc, *rest):
    lands = rest[: 4 * len(parts)]
    send, recv = rest[4 * len(parts) :]
    me = place()
    greet(me, sizes)
    keep = [[pl.ds(0, n) for n in sizes] for _ in parts]
    copies = []
    flying = [[] for _ in parts]

    def start(p, stage):
        low, rows = parts[p]
        dim = ORDERS[p][3 - stage]
        source = p_ref if stage == 0 else acc
        flying[p] = []
        for step in range(1, sizes[dim]):
            index = list(keep[p])
            index[dim] = lax.rem(me[dim] + step, sizes[dim])
            index = [pl.ds(i, 1) if not isinstance(i, pl.Slice) else i for i in index]
            copy = pltpu.make_async_remote_copy(
                src_ref=source.at[tuple(index) + (pl.ds(low, rows),)],
                dst_ref=lands[p * 4 + stage].at[step - 1],
                send_sem=send.at[p, stage, step - 1],
                recv_sem=recv.at[p, stage, step - 1],
                device_id=device(peer(me, sizes, dim, step)),
                device_id_type=MESH,
            )
            copy.start()
            flying[p].append(copy)
            copies.append(copy)
        keep[p][dim] = me[dim]

    def add(p, stage):
        low, rows = parts[p]
        for copy in flying[p]:
            copy.wait_recv()
        dim = ORDERS[p][3 - stage]
        source = p_ref if stage == 0 else acc
        land = lands[p * 4 + stage]
        shape = left_shape(sizes, ORDERS[p][::-1], stage)
        gone = ORDERS[p][::-1][: stage + 1]

        def body(j, carry):
            rest_index = []
            left = j
            for d in reversed(range(4)):
                rest_index.append(lax.rem(left, shape[d]))
                left = lax.div(left, shape[d])
            rest_index = rest_index[::-1]
            full = tuple(me[d] if d in gone else rest_index[d] for d in range(4))
            total = source[full + (pl.ds(low, rows),)].astype(jnp.float32)
            for step in range(1, sizes[dim]):
                total += land[(step - 1,) + tuple(rest_index)].astype(jnp.float32)
            total = total.astype(acc.dtype)
            if stage == 3:
                out_ref[pl.ds(low, rows), :] = total
            else:
                acc[full + (pl.ds(low, rows),)] = total
            return carry

        lax.fori_loop(0, math.prod(shape), body, 0)

    for p in range(len(parts)):
        start(p, 0)
    for stage in range(4):
        for p in range(len(parts)):
            add(p, stage)
            if stage < 3:
                start(p, stage + 1)
    for copy in copies:
        copy.wait_send()


def scatter(partial, sizes):
    block = partial.shape[4:]
    parts = split_rows(block[0])
    most = max(sizes) - 1
    lands = []
    for p, (_, rows) in enumerate(parts):
        order = ORDERS[p][::-1]
        for stage in range(4):
            shape = (sizes[order[stage]] - 1,) + left_shape(sizes, order, stage)
            lands.append(pltpu.VMEM(shape + (rows, block[1]), partial.dtype))
    vmem = pl.BlockSpec(memory_space=pltpu.VMEM)
    return pl.pallas_call(
        functools.partial(scatter_kernel, sizes, parts),
        out_shape=jax.ShapeDtypeStruct(block, partial.dtype),
        in_specs=[vmem],
        out_specs=vmem,
        scratch_shapes=[pltpu.VMEM(partial.shape, partial.dtype)]
        + lands
        + [
            pltpu.SemaphoreType.DMA((len(parts), 4, most)),
            pltpu.SemaphoreType.DMA((len(parts), 4, most)),
        ],
        compiler_params=pltpu.CompilerParams(
            collective_id=1, has_side_effects=True, vmem_limit_bytes=40 * 2**20
        ),
    )(partial)


def expert_kernel(
    x_ref, c_ref, s_ref, wg_ref, wu_ref, wd_ref,
    out_ref, din_ref, dc_ref, gg_ref, gu_ref, gd_ref, acc_o, acc_i,
):
    step = pl.program_id(1)
    dot = functools.partial(lax.dot_general, preferred_element_type=jnp.float32)
    nn = (((1,), (0,)), ((), ()))
    nt = (((1,), (1,)), ((), ()))
    tn = (((0,), (0,)), ((), ()))
    x = x_ref[0]
    weight = s_ref[0][:, :1]
    d_out = (c_ref[0].astype(jnp.float32) * weight).astype(jnp.bfloat16)
    gate = dot(x, wg_ref[0], nn)
    up = dot(x, wu_ref[0], nn)
    sig = jax.nn.sigmoid(gate)
    act = gate * sig
    hidden = (act * up).astype(jnp.bfloat16)
    out = dot(hidden, wd_ref[0], nn)
    d_hidden = dot(d_out, wd_ref[0], nt)
    d_gate = (d_hidden * up * sig * (1.0 + gate * (1.0 - sig))).astype(jnp.bfloat16)
    d_up = (d_hidden * act).astype(jnp.bfloat16)
    gd_ref[0] = dot(hidden, d_out, tn).astype(jnp.bfloat16)
    gg_ref[0] = dot(x, d_gate, tn).astype(jnp.bfloat16)
    gu_ref[0] = dot(x, d_up, tn).astype(jnp.bfloat16)
    d_in = dot(d_gate, wg_ref[0], nt) + dot(d_up, wu_ref[0], nt)

    @pl.when(step == 0)
    def _():
        acc_o[...] = out
        acc_i[...] = d_in

    @pl.when(step > 0)
    def _():
        acc_o[...] += out
        acc_i[...] += d_in

    @pl.when(step == pl.num_programs(1) - 1)
    def _():
        whole = acc_o[...]
        out_ref[0] = (whole * weight).astype(jnp.bfloat16)
        din_ref[0] = acc_i[...].astype(jnp.bfloat16)
        dot_rows = jnp.sum(whole * c_ref[0].astype(jnp.float32), axis=1, keepdims=True)
        dc_ref[0] = jnp.broadcast_to(dot_rows, dc_ref.shape[1:])


def experts(x, cot, weight, w_gate, w_up, w_down):
    local, rows, width = x.shape
    hid = w_gate.shape[2]
    part = min(hid, 256)
    row_spec = pl.BlockSpec((1, rows, width), lambda e, h: (e, 0, 0))
    small = pl.BlockSpec((1, rows, 128), lambda e, h: (e, 0, 0))
    wide = pl.BlockSpec((1, width, part), lambda e, h: (e, 0, h))
    tall = pl.BlockSpec((1, part, width), lambda e, h: (e, h, 0))
    return pl.pallas_call(
        expert_kernel,
        grid=(local, hid // part),
        out_shape=(
            jax.ShapeDtypeStruct(x.shape, jnp.bfloat16),
            jax.ShapeDtypeStruct(x.shape, jnp.bfloat16),
            jax.ShapeDtypeStruct((local, rows, 128), jnp.float32),
            jax.ShapeDtypeStruct(w_gate.shape, jnp.bfloat16),
            jax.ShapeDtypeStruct(w_up.shape, jnp.bfloat16),
            jax.ShapeDtypeStruct(w_down.shape, jnp.bfloat16),
        ),
        in_specs=[row_spec, row_spec, small, wide, wide, tall],
        out_specs=(row_spec, row_spec, small, wide, wide, tall),
        scratch_shapes=[
            pltpu.VMEM((rows, width), jnp.float32),
            pltpu.VMEM((rows, width), jnp.float32),
        ],
        compiler_params=pltpu.CompilerParams(vmem_limit_bytes=56 * 2**20),
    )(x, cot, weight, w_gate, w_up, w_down)


def on_device(tokens, routes, combine, w_gate, w_up, w_down, cotangent):
    groups = lax.axis_size("expert")
    section = lax.axis_size("section")
    sizes = sizes_of(groups, section)
    tok, feat = tokens.shape
    width = feat * section
    local = w_gate.shape[0]
    rows = -(-groups * CAP // 16) * 16
    block = jnp.concatenate([tokens, cotangent], axis=0).T
    info = jnp.concatenate([routes.astype(jnp.float32), combine], axis=1).T
    info = jnp.pad(info, ((0, 8 - 2 * TOPK), (0, 128 - tok)))
    gathered, infos = gather(block, info, sizes)
    gathered = gathered.reshape(groups, width, 2 * tok)
    ids = infos[:, :TOPK, :tok].astype(jnp.int32)
    weights = infos[:, TOPK : 2 * TOPK, :tok]
    named = (ids[..., None] == jnp.arange(local * groups, dtype=jnp.int32)).astype(jnp.int32)
    both = jnp.sum(named, axis=1)
    earlier = jnp.cumsum(both, axis=1) - both
    slot = jnp.sum(earlier[:, None] * named, axis=3)
    base = lax.axis_index("expert") * local
    group = jnp.arange(groups, dtype=jnp.int32)[:, None, None]
    code = (ids - base) * rows + group * CAP + slot
    hit = (code[None] == jnp.arange(local * rows, dtype=jnp.int32)[:, None, None, None]).astype(
        jnp.float32
    )
    pick = jnp.sum(hit, axis=2).astype(jnp.bfloat16)
    weight = jnp.sum(hit * weights[None], axis=(1, 2, 3))
    spread = functools.partial(jnp.einsum, "pet,edt->pd", preferred_element_type=jnp.float32)
    x = spread(pick, gathered[:, :, :tok]).astype(jnp.bfloat16).reshape(local, rows, width)
    cot = spread(pick, gathered[:, :, tok:]).astype(jnp.bfloat16).reshape(local, rows, width)
    weight = jnp.broadcast_to(weight.reshape(local, rows, 1), (local, rows, 128))
    out, d_in, d_rows, grad_gate, grad_up, grad_down = experts(
        x, cot, weight, w_gate, w_up, w_down
    )
    collect = functools.partial(jnp.einsum, "pet,pd->edt", preferred_element_type=jnp.float32)
    partial = jnp.concatenate(
        [
            collect(pick, out.reshape(local * rows, width)),
            collect(pick, d_in.reshape(local * rows, width)),
        ],
        axis=2,
    ).astype(jnp.bfloat16)
    d_rows = d_rows[:, :, 0].reshape(-1)
    d_combine = jnp.sum(hit * d_rows[:, None, None, None], axis=0)
    d_combine = lax.psum(d_combine, ("expert", "section"))
    d_combine = lax.dynamic_index_in_dim(
        d_combine, lax.axis_index("expert"), 0, keepdims=False
    ).T
    done = scatter(partial.reshape(sizes + (feat, 2 * tok)), sizes).T
    return (done[:tok], done[tok:], d_combine, grad_gate, grad_up, grad_down)


def solution(mesh):
    placed = (
        P("expert", "section"),
        P("expert", None),
        P("expert", None),
        P("expert", None, "section"),
        P("expert", None, "section"),
        P("expert", "section", None),
        P("expert", "section"),
    )
    return jax.shard_map(
        on_device,
        mesh=mesh,
        in_specs=placed,
        out_specs=(
            P("expert", "section"),
            P("expert", "section"),
            P("expert", None),
            P("expert", None, "section"),
            P("expert", None, "section"),
            P("expert", "section", None),
        ),
        check_vma=False,
    )
```

time: 304 us -> 137 us (0.45)
  waiting for transfers between devices: 114 us -> 0 us
  Pallas kernels: 0 us -> 77.7 us
  matrix products: 65.4 us -> 5.75 us
  blocking collectives: 73.9 us -> 39 us
  starting transfers between devices: 14.3 us -> 0 us
  between operations: 14.3 us -> 0.77 us
  local copies, waits for them, and re-layouts: 19.2 us -> 9.02 us
    unnamed x4 -> x0, waiting for transfers between devices: 96 us -> none
    pallas_call x0 -> x3, Pallas kernels: none -> 77.7 us  [the longest x1 37.4 us: experts(): pl.pallas_call(expert_kernel, grid=(local, hid // part), out_shape=(jax.S...]
    dot_general x13 -> x2, matrix products: 65.4 us -> 3.75 us  [the longest x1 2 us: on_device(): spread(pick, gathered[:, :, tok:]).astype(jnp.bfloat16)]
    all_gather x2 -> x0, blocking collectives: 43.9 us -> none  [spread(): whole = lax.all_gather(values, 'section', axis=1, tiled=True)]
    all_to_all x4 -> x0, waiting for transfers between devices: 18.1 us -> none  [the longest x2 14.8 us: spread(): lax.all_to_all(sent, 'expert', split_axis=0, concat_axis=1, tiled=True)]
    all_to_all x4 -> x0, starting transfers between devices: 13.8 us -> none  [the longest x2 7.21 us: spread(): lax.all_to_all(sent, 'expert', split_axis=0, concat_axis=1, tiled=True)]
    psum x1, blocking collectives: 30 us -> 39 us  [on_device(): d_combine = lax.psum(d_combine, ('expert', 'section'))]
    unnamed x27 -> x6, local copies, waits for them, and re-layouts: 11.7 us -> 3.69 us
  transfers between devices with their start and end apart: 6 -> 0, of which waited for: 4 -> 0; matrix products, arithmetic and copies ran while one was open for 13% -> 0% of each run, Pallas kernels for 0% -> 0%
where the time goes in v1:
time: 137 us; the launch traced here: 136 us
  Pallas kernels  77.7 us (57%)
  blocking collectives  39 us (28%)
  local copies, waits for them, and re-layouts  9.02 us (7%)
  matrix products  5.75 us (4%)
  other arithmetic  4.02 us (3%)
    psum x1, blocking collectives, on_device(): d_combine = lax.psum(d_combine, ('expert', 'section'))  39 us
    pallas_call x1, Pallas kernels, experts(): pl.pallas_call(expert_kernel, grid=(local, hid // part), out_shape=(jax.S...  37.4 us
    pallas_call x1, Pallas kernels, gather(): pl.pallas_call(functools.partial(gather_kernel, sizes, parts), out_shape=...  20.4 us
    pallas_call x1, Pallas kernels, scatter(): pl.pallas_call(functools.partial(scatter_kernel, sizes, parts), out_shape...  19.9 us
    unnamed x6, local copies, waits for them, and re-layouts  3.69 us

profile of v1, /device:TPU:0, one launch (start us, length us, event | category | flops | bytes accessed | tf_op | source)
XLA Modules:
  0.0 136.3 jit_solution(12315241583214274356)
XLA Ops:
  0.6 0.7 convert_element_type.25
  1.3 0.7 maximum_bitcast_fusion.1
  2.0 0.9 copy.29
  2.9 0.9 copy.30
  3.8 0.1 maximum_bitcast_fusion.x_ref
  3.9 20.4 %shard_map.118 = (bf16[2,4,2,2,192,128]{5,4,3,2,1,0:T(8,128)(2,1)S(1)}, f32[2,8,128]{2,1,0:T(8,128)S(1)}) custom-call(bf16[192,128]{1,0:T(8,128)(2,1)S(1)} %maximum_bitcast_fusion.x_ref, f32[8,128]{1,0:T(8,128)S(1)} %pad.4.info_ref), custom_call_target="tpu_custom_call" | custom-call | tf_op jit(solution)/shard_map/pallas_call | solution.py:113
  24.3 0.1 copy.31
  24.4 0.1 reduce_window_sum.11
  24.5 0.1 copy.33
  24.6 0.1 add_add_fusion
  24.7 0.1 select_reduce_fusion.1
  24.8 0.1 broadcast_in_dim.4
  24.9 0.7 broadcast_in_dim.5.s_ref
  25.7 2.0 %fusion.1 = bf16[192,3072]{1,0:T(8,128)(2,1)} fusion(bf16[192,2,64]{0,2,1:T(8,128)(2,1)S(1)} %get-tuple-element.41, bf16[2,3072,128]{2,1,0:T(8,128)(2,1)S(1)} %bitcast.38), kind=kOutput, calls=%fused_computation.3 | convolution fusion | flops 151584768 | bytes 2801664 | tf_op jit(solution)/shard_map/pet,edt->pd/dot_general | solution.py:341
  27.7 1.8 %fusion = bf16[192,3072]{1,0:T(8,128)(2,1)} fusion(bf16[192,2,64]{0,2,1:T(8,128)(2,1)S(1)} %get-tuple-element.41, bf16[2,3072,128]{2,1,0:T(8,128)(2,1)S(1)} %bitcast.39), kind=kOutput, calls=%fused_computation.2 | convolution fusion | flops 151584768 | bytes 2801664 | tf_op jit(solution)/shard_map/pet,edt->pd/dot_general | solution.py:340
  29.4 37.4 %shard_map.119 = (bf16[4,48,3072]{2,1,0:T(8,128)(2,1)}, bf16[4,48,3072]{2,1,0:T(8,128)(2,1)}, f32[4,48,128]{2,1,0:T(8,128)}, bf16[4,3072,512]{2,1,0:T(8,128)(2,1...) custom-call(bf16[4,48,3072]{2,1,0:T(8,128)(2,1)} %bitcast.46, bf16[4,48,3072]{2,1,0:T(8,128)(2,1)} %bitcast.45, ...), custom_call_target="tpu_custom_call" | custom-call | tf_op jit(solution)/shard_map/pallas_call | solution.py:291
  66.8 1.0 slice_reduce_fusion
  67.8 0.1 mul.51
  67.9 0.2 select_reduce_fusion
  68.1 39.0 %psum.7 = f32[2,2,64]{2,1,0:T(2,128)S(1)} all-reduce(f32[2,2,64]{2,1,0:T(2,128)S(1)} %select_reduce_fusion), channel_id=1, replica_groups=mesh['section'=16,'expert'=2] {'expert','section'}, use_global_device_ids=true, to_apply=%region_6.7 | all-reduce | flops 256 | bytes 2048 | tf_op jit(solution)/shard_map/psum | solution.py:356
  107.1 0.6 dynamic-slice_bitcast_fusion
  107.7 1.6 %fusion.6 = f32[3072,128]{0,1:S(1)} fusion(bf16[192,128]{0,1:T(8,128)(2,1)S(1)} %bitcast.47, bf16[192,3072]{1,0:T(8,128)(2,1)} %bitcast.50), kind=kOutput, calls=%fused_computation.25 | convolution fusion | flops 150994944 | bytes 2801664
  109.3 0.0 copy-start
  109.3 1.0 convert_bitcast_fusion
  110.3 0.5 copy-done
  110.9 0.4 fusion.5
  111.2 0.1 convert_bitcast_fusion.1
  111.3 0.9 copy.36
  112.2 1.8 %copy.37 = bf16[2,3072,64]{2,1,0:T(8,128)(2,1)S(1)} copy(bf16[2,3072,64]{1,2,0:T(8,128)(2,1)} %convert_bitcast_fusion) | data formatting | bytes 1572864 | tf_op jit(solution)/shard_map/pet,pd->edt/transpose | solution.py:350
  114.0 0.9 pad_maximum_fusion.p_ref
  114.8 19.9 %shard_map.120 = bf16[192,128]{1,0:T(8,128)(2,1)S(1)} custom-call(bf16[2,4,2,2,192,128]{5,4,3,2,1,0:T(8,128)(2,1)S(1)} %pad_maximum_fusion.p_ref), custom_call_target="tpu_custom_call" | custom-call | tf_op jit(solution)/shard_map/pallas_call | solution.py:221
  134.8 0.1 fusion.4
  134.8 0.7 copy.39
  135.5 0.7 copy.38
  (6 shorter events, 0.1 us)
Async XLA Ops:
  109.3 1.6 %copy-start = (bf16[4,48,3072]{2,1,0:T(8,128)(2,1)S(1)}, bf16[4,48,3072]{2,1,0:T(8,128)(2,1)}, u32[]{:S(2)}) copy-start(bf16[4,48,3072]{2,1,0:T(8,128)(2,1)} %get-tuple-element.16) | copy-start | bytes 3538948

commit v2 on v1

--- a/solution.py
+++ b/solution.py
@@ -57,9 +57,19 @@
     return ((0, rows),)
 
 
-def gather_kernel(sizes, parts, x_ref, info_ref, out_ref, info_out, send, recv, isend, irecv):
+def eye(n):
+    row = lax.broadcasted_iota(jnp.int32, (n, n), 0)
+    col = lax.broadcasted_iota(jnp.int32, (n, n), 1)
+    return jnp.where(row == col, 1.0, 0.0).astype(jnp.bfloat16)
+
+
+def gather_kernel(sizes, parts, tok_ref, cot_ref, info_ref, out_ref, info_out, send, recv, isend, irecv):
     me = place()
-    out_ref[me[0], me[1], me[2], me[3]] = x_ref[...]
+    both = jnp.concatenate([tok_ref[...], cot_ref[...]], axis=0)
+    turned = lax.dot_general(
+        both, eye(both.shape[0]), (((0,), (0,)), ((), ())), preferred_element_type=jnp.float32
+    )
+    out_ref[me[0], me[1], me[2], me[3]] = turned.astype(jnp.bfloat16)
     info_out[me[EX]] = info_ref[...]
     greet(me, sizes)
     copies = []
@@ -105,18 +115,18 @@
         copy.wait_send()
 
 
-def gather(block, info, sizes):
-    rows = block.shape[0]
+def gather(tokens, cotangent, info, sizes):
+    rows = tokens.shape[1]
     parts = split_rows(rows)
     most = max(sizes) - 1
     vmem = pl.BlockSpec(memory_space=pltpu.VMEM)
     return pl.pallas_call(
         functools.partial(gather_kernel, sizes, parts),
         out_shape=(
-            jax.ShapeDtypeStruct(sizes + block.shape, block.dtype),
+            jax.ShapeDtypeStruct(sizes + (rows, 2 * tokens.shape[0]), tokens.dtype),
             jax.ShapeDtypeStruct((sizes[EX],) + info.shape, info.dtype),
         ),
-        in_specs=[vmem, vmem],
+        in_specs=[vmem, vmem, vmem],
         out_specs=(vmem, vmem),
         scratch_shapes=[
             pltpu.SemaphoreType.DMA((len(parts), 4, most)),
@@ -127,7 +137,7 @@
         compiler_params=pltpu.CompilerParams(
             collective_id=0, has_side_effects=True, vmem_limit_bytes=40 * 2**20
         ),
-    )(block, info)
+    )(tokens, cotangent, info)
 
 
 def left_shape(sizes, order, stage):
@@ -135,10 +145,12 @@
     return tuple(1 if d in gone else sizes[d] for d in range(4))
 
 
-def scatter_kernel(sizes, parts, p_ref, out_ref, acc, *rest):
+def scatter_kernel(sizes, parts, p_ref, dc_ref, mixed_ref, dtok_ref, dc_out, acc, out_ref, *rest):
     lands = rest[: 4 * len(parts)]
-    send, recv = rest[4 * len(parts) :]
+    small = rest[4 * len(parts) : 4 * len(parts) + 4]
+    send, recv, ssend, srecv = rest[4 * len(parts) + 4 :]
     me = place()
+    small[0][me[ORDERS[0][3]]] = dc_ref[...]
     greet(me, sizes)
     keep = [[pl.ds(0, n) for n in sizes] for _ in parts]
     copies = []
@@ -196,18 +208,58 @@
 
         lax.fori_loop(0, math.prod(shape), body, 0)
 
+    def start_small(stage):
+        dim = ORDERS[0][3 - stage]
+        block = small[stage].at[me[dim]]
+        started = []
+        for step in range(1, sizes[dim]):
+            copy = pltpu.make_async_remote_copy(
+                src_ref=block,
+                dst_ref=block,
+                send_sem=ssend.at[stage, step - 1],
+                recv_sem=srecv.at[stage, step - 1],
+                device_id=device(peer(me, sizes, dim, step)),
+                device_id_type=MESH,
+            )
+            copy.start()
+            started.append(copy)
+            copies.append(copy)
+        return started
+
+    def add_small(stage, started):
+        for copy in started:
+            copy.wait_recv()
+        total = small[stage][0]
+        for i in range(1, sizes[ORDERS[0][3 - stage]]):
+            total += small[stage][i]
+        if stage == 3:
+            dc_out[...] = total
+        else:
+            small[stage + 1][me[ORDERS[0][2 - stage]]] = total
+
     for p in range(len(parts)):
         start(p, 0)
+    started = start_small(0)
     for stage in range(4):
         for p in range(len(parts)):
             add(p, stage)
             if stage < 3:
                 start(p, stage + 1)
+        add_small(stage, started)
+        if stage < 3:
+            started = start_small(stage + 1)
+    block = out_ref[...]
+    turned = lax.dot_general(
+        eye(block.shape[1]), block, (((1,), (1,)), ((), ())), preferred_element_type=jnp.float32
+    ).astype(jnp.bfloat16)
+    tok = mixed_ref.shape[0]
+    mixed_ref[...] = turned[:tok]
+    dtok_ref[...] = turned[tok:]
     for copy in copies:
         copy.wait_send()
 
 
-def scatter(partial, sizes):
+def scatter(partial, d_combine, sizes):
     block = partial.shape[4:]
     parts = split_rows(block[0])
     most = max(sizes) - 1
@@ -220,33 +272,80 @@
     vmem = pl.BlockSpec(memory_space=pltpu.VMEM)
     return pl.pallas_call(
         functools.partial(scatter_kernel, sizes, parts),
-        out_shape=jax.ShapeDtypeStruct(block, partial.dtype),
-        in_specs=[vmem],
-        out_specs=vmem,
-        scratch_shapes=[pltpu.VMEM(partial.shape, partial.dtype)]
+        out_shape=(
+            jax.ShapeDtypeStruct((block[1] // 2, block[0]), partial.dtype),
+            jax.ShapeDtypeStruct((block[1] // 2, block[0]), partial.dtype),
+            jax.ShapeDtypeStruct(d_combine.shape, d_combine.dtype),
+        ),
+        in_specs=[vmem, vmem],
+        out_specs=(vmem, vmem, vmem),
+        scratch_shapes=[
+            pltpu.VMEM(partial.shape, partial.dtype),
+            pltpu.VMEM(block, partial.dtype),
+        ]
         + lands
+        + [
+            pltpu.VMEM((sizes[ORDERS[0][3 - stage]],) + d_combine.shape, d_combine.dtype)
+            for stage in range(4)
+        ]
         + [
             pltpu.SemaphoreType.DMA((len(parts), 4, most)),
             pltpu.SemaphoreType.DMA((len(parts), 4, most)),
+            pltpu.SemaphoreType.DMA((4, most)),
+            pltpu.SemaphoreType.DMA((4, most)),
         ],
         compiler_params=pltpu.CompilerParams(
             collective_id=1, has_side_effects=True, vmem_limit_bytes=40 * 2**20
         ),
-    )(partial)
+    )(partial, d_combine)
 
 
 def expert_kernel(
-    x_ref, c_ref, s_ref, wg_ref, wu_ref, wd_ref,
-    out_ref, din_ref, dc_ref, gg_ref, gu_ref, gd_ref, acc_o, acc_i,
+    code_ref, comb_ref, all_ref, wg_ref, wu_ref, wd_ref,
+    part_ref, dc_ref, gg_ref, gu_ref, gd_ref,
+    x_ref, back_ref, d_ref, w_ref, r_ref, acc_o, acc_i,
 ):
-    step = pl.program_id(1)
+    expert, step = pl.program_id(0), pl.program_id(1)
+    last = pl.num_programs(1) - 1
     dot = functools.partial(lax.dot_general, preferred_element_type=jnp.float32)
     nn = (((1,), (0,)), ((), ()))
     nt = (((1,), (1,)), ((), ()))
     tn = (((0,), (0,)), ((), ()))
-    x = x_ref[0]
-    weight = s_ref[0][:, :1]
-    d_out = (c_ref[0].astype(jnp.float32) * weight).astype(jnp.bfloat16)
+    groups = all_ref.shape[0]
+    _, local, rows, width = x_ref.shape
+    lanes = all_ref.shape[2]
+    every = local * rows
+    row = lax.broadcasted_iota(jnp.int32, (every, lanes), 0)
+    lane = lax.broadcasted_iota(jnp.int32, (every, lanes), 1)
+
+    def hits(g):
+        return jnp.where(code_ref[g] == row, 1.0, 0.0)
+
+    def picks(g):
+        hit = hits(g)
+        pick = hit + pltpu.roll(hit, lanes // 2, 1)
+        first = jnp.where(lane < lanes // 2, pick, 0.0)
+        return jnp.concatenate([first, pick - first], axis=0).astype(jnp.bfloat16)
+
+    @pl.when((step == 0) & (expert == 0))
+    def _():
+        weight = jnp.zeros((every, 1), jnp.float32)
+        for g in range(groups):
+            weight += jnp.sum(hits(g) * comb_ref[g], axis=1, keepdims=True)
+        w_ref[...] = jnp.broadcast_to(weight, (every, lanes)).reshape(w_ref.shape)
+        found = dot(picks(0), all_ref[0], nt)
+        for g in range(1, groups):
+            found += dot(picks(g), all_ref[g], nt)
+        x_ref[...] = found.astype(jnp.bfloat16).reshape(x_ref.shape)
+
+    @pl.when(step == 0)
+    def _():
+        d_ref[...] = (
+            x_ref[1, expert].astype(jnp.float32) * w_ref[expert][:, :1]
+        ).astype(jnp.bfloat16)
+
+    x = x_ref[0, expert]
+    d_out = d_ref[...]
     gate = dot(x, wg_ref[0], nn)
     up = dot(x, wu_ref[0], nn)
     sig = jax.nn.sigmoid(gate)
@@ -271,56 +370,69 @@
         acc_o[...] += out
         acc_i[...] += d_in
 
-    @pl.when(step == pl.num_programs(1) - 1)
+    @pl.when(step == last)
     def _():
         whole = acc_o[...]
-        out_ref[0] = (whole * weight).astype(jnp.bfloat16)
-        din_ref[0] = acc_i[...].astype(jnp.bfloat16)
-        dot_rows = jnp.sum(whole * c_ref[0].astype(jnp.float32), axis=1, keepdims=True)
-        dc_ref[0] = jnp.broadcast_to(dot_rows, dc_ref.shape[1:])
-
-
-def experts(x, cot, weight, w_gate, w_up, w_down):
-    local, rows, width = x.shape
-    hid = w_gate.shape[2]
+        back_ref[0, expert] = (whole * w_ref[expert][:, :1]).astype(jnp.bfloat16)
+        back_ref[1, expert] = acc_i[...].astype(jnp.bfloat16)
+        dot_rows = jnp.sum(whole * x_ref[1, expert].astype(jnp.float32), axis=1, keepdims=True)
+        r_ref[expert] = jnp.broadcast_to(dot_rows, r_ref.shape[1:])
+
+    @pl.when((step == last) & (expert == local - 1))
+    def _():
+        stack = back_ref[...].reshape(2 * every, width)
+        drow = r_ref[...].reshape(every, lanes)
+        for g in range(groups):
+            part_ref[g] = dot(stack, picks(g), tn).astype(jnp.bfloat16)
+            dc_ref[g] = jnp.sum(hits(g) * drow, axis=0, keepdims=True)
+
+
+def experts(code, comb, gathered, rows, w_gate, w_up, w_down):
+    groups, width, lanes = gathered.shape
+    local, _, hid = w_gate.shape
     part = min(hid, 256)
-    row_spec = pl.BlockSpec((1, rows, width), lambda e, h: (e, 0, 0))
-    small = pl.BlockSpec((1, rows, 128), lambda e, h: (e, 0, 0))
+    whole = lambda shape: pl.BlockSpec(shape, lambda e, h: (0,) * len(shape))
     wide = pl.BlockSpec((1, width, part), lambda e, h: (e, 0, h))
     tall = pl.BlockSpec((1, part, width), lambda e, h: (e, h, 0))
     return pl.pallas_call(
         expert_kernel,
         grid=(local, hid // part),
         out_shape=(
-            jax.ShapeDtypeStruct(x.shape, jnp.bfloat16),
-            jax.ShapeDtypeStruct(x.shape, jnp.bfloat16),
-            jax.ShapeDtypeStruct((local, rows, 128), jnp.float32),
+            jax.ShapeDtypeStruct(gathered.shape, jnp.bfloat16),
+            jax.ShapeDtypeStruct((groups, 1, lanes), jnp.float32),
             jax.ShapeDtypeStruct(w_gate.shape, jnp.bfloat16),
             jax.ShapeDtypeStruct(w_up.shape, jnp.bfloat16),
             jax.ShapeDtypeStruct(w_down.shape, jnp.bfloat16),
         ),
-        in_specs=[row_spec, row_spec, small, wide, wide, tall],
-        out_specs=(row_spec, row_spec, small, wide, wide, tall),
+        in_specs=[
+            whole(code.shape), whole(comb.shape), whole(gathered.shape), wide, wide, tall,
+        ],
+        out_specs=(
+            whole(gathered.shape), whole((groups, 1, lanes)), wide, wide, tall,
+        ),
         scratch_shapes=[
+            pltpu.VMEM((2, local, rows, width), jnp.bfloat16),
+            pltpu.VMEM((2, local, rows, width), jnp.bfloat16),
+            pltpu.VMEM((rows, width), jnp.bfloat16),
+            pltpu.VMEM((local, rows, lanes), jnp.float32),
+            pltpu.VMEM((local, rows, lanes), jnp.float32),
             pltpu.VMEM((rows, width), jnp.float32),
             pltpu.VMEM((rows, width), jnp.float32),
         ],
-        compiler_params=pltpu.CompilerParams(vmem_limit_bytes=56 * 2**20),
-    )(x, cot, weight, w_gate, w_up, w_down)
+        compiler_params=pltpu.CompilerParams(vmem_limit_bytes=58 * 2**20),
+    )(code, comb, gathered, w_gate, w_up, w_down)
 
 
 def on_device(tokens, routes, combine, w_gate, w_up, w_down, cotangent):
     groups = lax.axis_size("expert")
-    section = lax.axis_size("section")
-    sizes = sizes_of(groups, section)
+    sizes = sizes_of(groups, lax.axis_size("section"))
     tok, feat = tokens.shape
-    width = feat * section
+    width = feat * lax.axis_size("section")
     local = w_gate.shape[0]
     rows = -(-groups * CAP // 16) * 16
-    block = jnp.concatenate([tokens, cotangent], axis=0).T
     info = jnp.concatenate([routes.astype(jnp.float32), combine], axis=1).T
     info = jnp.pad(info, ((0, 8 - 2 * TOPK), (0, 128 - tok)))
-    gathered, infos = gather(block, info, sizes)
+    gathered, infos = gather(tokens, cotangent, info, sizes)
     gathered = gathered.reshape(groups, width, 2 * tok)
     ids = infos[:, :TOPK, :tok].astype(jnp.int32)
     weights = infos[:, TOPK : 2 * TOPK, :tok]
@@ -331,34 +443,21 @@
     base = lax.axis_index("expert") * local
     group = jnp.arange(groups, dtype=jnp.int32)[:, None, None]
     code = (ids - base) * rows + group * CAP + slot
-    hit = (code[None] == jnp.arange(local * rows, dtype=jnp.int32)[:, None, None, None]).astype(
-        jnp.float32
-    )
-    pick = jnp.sum(hit, axis=2).astype(jnp.bfloat16)
-    weight = jnp.sum(hit * weights[None], axis=(1, 2, 3))
-    spread = functools.partial(jnp.einsum, "pet,edt->pd", preferred_element_type=jnp.float32)
-    x = spread(pick, gathered[:, :, :tok]).astype(jnp.bfloat16).reshape(local, rows, width)
-    cot = spread(pick, gathered[:, :, tok:]).astype(jnp.bfloat16).reshape(local, rows, width)
-    weight = jnp.broadcast_to(weight.reshape(local, rows, 1), (local, rows, 128))
-    out, d_in, d_rows, grad_gate, grad_up, grad_down = experts(
-        x, cot, weight, w_gate, w_up, w_down
-    )
-    collect = functools.partial(jnp.einsum, "pet,pd->edt", preferred_element_type=jnp.float32)
-    partial = jnp.concatenate(
-        [
-            collect(pick, out.reshape(local * rows, width)),
-            collect(pick, d_in.reshape(local * rows, width)),
-        ],
-        axis=2,
-    ).astype(jnp.bfloat16)
-    d_rows = d_rows[:, :, 0].reshape(-1)
-    d_combine = jnp.sum(hit * d_rows[:, None, None, None], axis=0)
-    d_combine = lax.psum(d_combine, ("expert", "section"))
+    code = code.reshape(groups, 1, TOPK * tok)
+    comb = weights.reshape(groups, 1, TOPK * tok)
+    partial, d_combine, grad_gate, grad_up, grad_down = experts(
+        code, comb, gathered, rows, w_gate, w_up, w_down
+    )
+    short = -(-groups // 8) * 8
+    d_combine = jnp.pad(d_combine[:, 0], ((0, short - groups), (0, 0)))
+    mixed, d_tokens, d_combine = scatter(
+        partial.reshape(sizes + (feat, 2 * tok)), d_combine, sizes
+    )
     d_combine = lax.dynamic_index_in_dim(
         d_combine, lax.axis_index("expert"), 0, keepdims=False
-    ).T
-    done = scatter(partial.reshape(sizes + (feat, 2 * tok)), sizes).T
-    return (done[:tok], done[tok:], d_combine, grad_gate, grad_up, grad_down)
+    )
+    d_combine = d_combine.reshape(TOPK, tok).T
+    return (mixed, d_tokens, d_combine, grad_gate, grad_up, grad_down)
 
 
 def solution(mesh):

time: 137 us -> 94 us (0.69)
  blocking collectives: 39 us -> 0 us
  matrix products: 5.75 us -> 0 us
  Pallas kernels: 77.7 us -> 83.3 us
  other arithmetic: 4.02 us -> 1.6 us
    psum x1 -> x0, blocking collectives: 39 us -> none  [on_device(): d_combine = lax.psum(d_combine, ('expert', 'section'))]
    dot_general x2 -> x0, matrix products: 3.75 us -> none  [the longest x1 2 us: on_device(): spread(pick, gathered[:, :, tok:]).astype(jnp.bfloat16)]
    pallas_call x1, Pallas kernels: 37.4 us -> 40.9 us  [experts(): pl.pallas_call(expert_kernel, grid=(local, hid // part), out_shape=(jax.S...]
    transpose x3 -> x0, local copies, waits for them, and re-layouts: 3.2 us -> none  [the longest x1 1.78 us: on_device(): collect(pick, d_in.reshape(local * rows, width))]
    pallas_call x1, Pallas kernels: 19.9 us -> 21.9 us  [scatter(): pl.pallas_call(functools.partial(scatter_kernel, sizes, parts), out_shape...]
    unnamed x2 -> x0, matrix products: 1.99 us -> none
    reshape x0 -> x3, local copies, waits for them, and re-layouts: none -> 1.93 us  [the longest x1 0.65 us: on_device(): code = code.reshape(groups, 1, TOPK * tok)]
    unnamed x6 -> x10, local copies, waits for them, and re-layouts: 3.69 us -> 5.29 us
where the time goes in v2:
time: 94 us; the launch traced here: 93.7 us
  Pallas kernels  83.3 us (89%)
  local copies, waits for them, and re-layouts  8.1 us (9%)
  other arithmetic  1.6 us (2%)
    pallas_call x1, Pallas kernels, experts(): pl.pallas_call(expert_kernel, grid=(local, hid // part), out_shape=(jax.S...  40.9 us
    pallas_call x1, Pallas kernels, scatter(): pl.pallas_call(functools.partial(scatter_kernel, sizes, parts), out_shape...  21.9 us
    pallas_call x1, Pallas kernels, gather(): pl.pallas_call(functools.partial(gather_kernel, sizes, parts), out_shape=...  20.5 us
    unnamed x10, local copies, waits for them, and re-layouts  5.29 us

profile of v2, /device:TPU:0, one launch (start us, length us, event | category | flops | bytes accessed | tf_op | source)
XLA Modules:
  0.0 93.7 jit_solution(8737674516448343703)
XLA Ops:
  0.6 0.7 convert_element_type.13
  1.3 0.7 maximum_bitcast_fusion
  2.0 0.0 copy-start.2
  2.0 0.7 copy-done.2
  2.8 0.0 copy-start.3
  2.8 0.8 copy-done.3
  3.5 20.5 %shard_map.118 = (bf16[2,4,2,2,192,128]{5,4,3,2,1,0:T(8,128)(2,1)S(1)}, f32[2,8,128]{2,1,0:T(8,128)S(1)}) custom-call(bf16[64,192]{1,0:T(8,128)(2,1)S(1)} %copy-done.2, bf16[64,192]{1,0:T(8,128)(2,1)S(1)} %copy-done.3, f32[8,128]{1,0:T(8,128)S(1)} %pad.8.info_ref), custom_call_target="tpu_custom_call" | custom-call | tf_op jit(solution)/shard_map/pallas_call | solution.py:123
  24.1 0.0 copy-start
  24.1 1.1 %copy-done = bf16[2,4,2,2,192,128]{5,4,3,2,1,0:T(8,128)(2,1)} copy-done((bf16[2,4,2,2,192,128]{5,4,3,2,1,0:T(8,128)(2,1)}, bf16[2,4,2,2,192,128]{5,4,3,2,1,0:T(8,128)(2,1)S(1)}, u32[]{:S(2)}) %copy-start) | copy-done | bytes 1572888
  25.3 0.6 reshape.44.comb_ref
  25.9 0.1 copy.13
  26.0 0.1 reduce_window_sum.11
  26.1 0.1 copy.15
  26.2 0.1 add_add_fusion
  26.3 0.6 reshape.43.code_ref
  26.9 40.9 %shard_map.119 = (bf16[2,3072,128]{2,1,0:T(8,128)(2,1)}, f32[2,1,128]{2,1,0:T(1,128)}, bf16[4,3072,512]{2,1,0:T(8,128)(2,1)}, bf16[4,3072,512]{2,1,0:T(8,128)(2,1)}, bf16[4,512,3072]{2,1,0:T(8,128)(2,1)}) custom-call(s32[2,1,128]{2,1,0:T(1,128)} %reshape.43.code_ref, f32[2,1,128]{2,1,0:T(1,128)} %reshape.44.comb_ref, bf16[2,3072,128]{2,1,0:T(8,128)(2,1)} %bitcast.6, ...), custom_call_target="tpu_custom_call" | custom-call | tf_op jit(solution)/shard_map/pallas_call | solution.py:397
  67.8 0.7 pad.9.dc_ref
  68.5 0.0 copy-start.1
  68.5 1.4 %copy-done.1 = bf16[2,3072,128]{2,1,0:T(8,128)(2,1)S(1)} copy-done((bf16[2,3072,128]{2,1,0:T(8,128)(2,1)S(1)}, bf16[2,3072,128]{2,1,0:T(8,128)(2,1)}, u32[]{:S(2)}) %copy-start.1) | copy-done | bytes 1572888
  69.9 21.9 %shard_map.120 = (bf16[64,192]{1,0:T(8,128)(2,1)S(1)}, bf16[64,192]{1,0:T(8,128)(2,1)S(1)}, f32[8,128]{1,0:T(8,128)S(1)}) custom-call(bf16[2,4,2,2,192,128]{5,4,3,2,1,0:T(8,128)(2,1)S(1)} %bitcast.7, f32[8,128]{1,0:T(8,128)S(1)} %pad.9.dc_ref), custom_call_target="tpu_custom_call" | custom-call | tf_op jit(solution)/shard_map/pallas_call | solution.py:273
  91.8 0.6 reshape.47
  92.5 0.6 copy.18
  93.1 0.6 copy.19
  (7 shorter events, 0.1 us)
Async XLA Ops:
  2.0 0.8 copy-start.2
  2.8 0.8 copy-start.3
  24.1 1.2 %copy-start = (bf16[2,4,2,2,192,128]{5,4,3,2,1,0:T(8,128)(2,1)}, bf16[2,4,2,2,192,128]{5,4,3,2,1,0:T(8,128)(2,1)S(1)}, u32[]{:S(2)}) copy-start(bf16[2,4,2,2,192,128]{5,4,3,2,1,0:T(8,128)(2,1)S(1)} %get-tuple-element.17) | copy-start | bytes 4718596
  68.5 1.4 %copy-start.1 = (bf16[2,3072,128]{2,1,0:T(8,128)(2,1)S(1)}, bf16[2,3072,128]{2,1,0:T(8,128)(2,1)}, u32[]{:S(2)}) copy-start(bf16[2,3072,128]{2,1,0:T(8,128)(2,1)} %get-tuple-element.18) | copy-start | bytes 4718596
